TPU v7x, 32 devices: a whole 2x2x4 slice. The times are simulated.
32 devices in a mesh: wide: 16 (over z, y, x), narrow: 2 (over core).
Axes of the slice: x: 2, y: 2, z: 4, core: 2. Of those that a mesh axis runs over, the one named last changes fastest.
Arguments:
- effects_start: float32 [16384, 256], P(('wide', 'narrow')), may hold values from -3 to 3
- marginal: float32 [16384, 256], P(('wide', 'narrow')), may hold values from -6 to 6
- ld_diag: float32 [16384, 512], P(('wide', 'narrow')), may hold values from -1 to 1, as said below
- ld_upper: float32 [16384, 512], P(('wide', 'narrow')), may hold values from -1 to 1
- penalty_grid: float32 [16], replicated, may hold values from 0.1 to 1
- penalty_index: int32 [256], replicated, may hold values from 0 to 15
- dosages: bfloat16 [64, 16384], P(None, ('wide', 'narrow')), may hold values from 0 to 2
- stack_weights: float32 [256, 256], replicated, may hold values from -0.375 to 0.375
Outputs:
- effects: float32 [16384, 256], P(('wide', 'narrow'))
- stacked: float32 [64, 256], P(('wide', 'narrow'))
Inputs may be any that keep to these rules, and one draw needn't show every extreme that they name: `ld_diag`: each diagonal tile is symmetric.
All inputs are finite; a program needn't handle non-finite values.
Results may differ from a plain program's by a relative error of at most 0.0037.
Values sent between devices are 32-bit elements; how exact they have to be, the bound alone decides.
A program may use at most 64 MiB of HBM per device.

v0:
```python
import math

import jax
import jax.numpy as jnp
from jax import lax
from jax.sharding import PartitionSpec as P

ITERS = 3


step_size = 0.5


def passed_along(block, axis, distance):
    devices = range(lax.axis_size(axis))
    route = [(i - distance, i) for i in devices if i - distance in devices]
    return lax.ppermute(block, axis, route)


def full_dot(left, right):
    return jnp.dot(left, right, precision=lax.Precision.HIGHEST, preferred_element_type=jnp.float32)


def transposed_dot(left, right):
    return lax.dot_general(
        left,
        right,
        (((0,), (0,)), ((), ())),
        precision=lax.Precision.HIGHEST,
        preferred_element_type=jnp.float32,
    )


def shards(
    effects_start, marginal, ld_diag, ld_upper, penalty_grid, penalty_index, dosages, stack_weights
):
    variants = ld_diag.shape[0]
    levels = penalty_grid.shape[0]
    picked = (penalty_index[None, :] == jnp.arange(levels, dtype=jnp.int32)[:, None]).astype(
        jnp.float32
    )
    threshold = step_size * jnp.sum(picked * penalty_grid[:, None], axis=0)
    effects = effects_start
    for sweep in range(ITERS):
        own_term = full_dot(ld_diag, effects)
        next_rows = passed_along(effects, ("wide", "narrow"), -1)
        handed = transposed_dot(ld_upper, effects)
        from_prev = passed_along(handed, ("wide", "narrow"), 1)
        coupled = full_dot(ld_upper, next_rows) + from_prev
        gradient = own_term + coupled - marginal
        moved = effects - step_size * gradient
        effects = jnp.sign(moved) * jnp.maximum(jnp.abs(moved) - threshold[None, :], 0.0)
    effects_low = effects.astype(jnp.bfloat16)
    wide_count = lax.axis_size("wide")
    narrow_count = lax.axis_size("narrow")
    shrink = 1.0 / math.sqrt(variants * wide_count * narrow_count)
    owner_block = lax.psum_scatter(
        jnp.dot(dosages, effects_low, preferred_element_type=jnp.float32),
        "wide",
        scatter_dimension=0,
        tiled=True,
    )
    summed = lax.psum_scatter(owner_block, "narrow", scatter_dimension=0, tiled=True)
    scores = summed * shrink
    stacked = full_dot(scores, stack_weights)
    return (effects, stacked)


def solution(mesh):
    return jax.shard_map(
        shards,
        mesh=mesh,
        in_specs=(
            P(("wide", "narrow"), None),
            P(("wide", "narrow"), None),
            P(("wide", "narrow"), None),
            P(("wide", "narrow"), None),
            P(),
            P(),
            P(None, ("wide", "narrow")),
            P(),
        ),
        out_specs=(P(("wide", "narrow"), None), P(("wide", "narrow"), None)),
        check_vma=False,
    )
```

profile of v0, /device:TPU:0, one launch (start us, length us, event | category | flops | bytes accessed | tf_op | source)
XLA Modules:
  0.0 185.0 jit_solution(16473996380125695901)
XLA Ops:
  7.2 0.0 copy-start
  7.2 0.0 all-reduce.4.cloned.1.call-start
  7.3 1.4 collective-permute-start
  8.7 2.9 %fusion.20 = f32[512,256]{1,0:T(8,128)S(1)} fusion(f32[512,512]{1,0:T(8,128)S(1)} %copy-done, f32[512,256]{1,0:T(8,128)} %param.8), kind=kOutput, calls=%fused_computation.36 | convolution fusion | flops 805306368 | bytes 2097152 | tf_op jit(solution)/shard_map/dot_general | solution.py:25
  11.6 3.1 %collective-permute-start.1 = (f32[512,256]{1,0:T(8,128)S(1)}, f32[512,256]{1,0:T(8,128)S(1)}, u32[]{:S(2)}, u32[]{:S(2)}) collective-permute-start(f32[512,256]{1,0:T(8,128)S(1)} %fusion.20), channel_id=1, source_target_pairs={{0,1},{1,2},{2,3},{3,4},{4,5},{5,6},{6,7},{7,8},{8,9},{9,10},{10,1... | collective-permute-start | bytes 1572872 | tf_op jit(solution)/shard_map/ppermute | solution.py:17
  14.7 0.1 select_reduce_fusion
  14.8 1.0 fusion.19
  15.8 0.4 collective-permute-done.1
  16.1 1.2 maximum_multiply_fusion.2
  17.3 1.8 convolution_bitcast_fusion.3
  19.2 12.0 %collective-permute-start.3 = (f32[512,256]{1,0:T(8,128)S(1)}, f32[512,256]{1,0:T(8,128)S(1)}, u32[]{:S(2)}, u32[]{:S(2)}) collective-permute-start(f32[512,256]{1,0:T(8,128)S(1)} %convolution_bitcast_fusion.3), channel_id=1, source_target_pairs={{0,1},{1,2},{2,3},{3,4},{4,5},{5,6},{6,7},{7,8},{8,9},{9,10},{10,1... | collective-permute-start | bytes 1572872 | tf_op jit(solution)/shard_map/ppermute | solution.py:17
  31.1 1.3 collective-permute-start.2
  32.4 1.0 convolution_bitcast_fusion.5
  33.5 3.4 %collective-permute-done.2 = f32[512,256]{1,0:T(8,128)S(1)} collective-permute-done((f32[512,256]{1,0:T(8,128)S(1)}, f32[512,256]{1,0:T(8,128)S(1)}, u32[]{:S(2)}, u32[]{:S(2)}) %collective-permute-start.2) | collective-permute-done | bytes 524320 | tf_op jit(solution)/shard_map/ppermute | solution.py:17
  36.9 1.2 maximum_multiply_fusion.1
  38.1 1.8 convolution_bitcast_fusion
  40.0 10.9 %collective-permute-start.5 = (f32[512,256]{1,0:T(8,128)S(1)}, f32[512,256]{1,0:T(8,128)S(1)}, u32[]{:S(2)}, u32[]{:S(2)}) collective-permute-start(f32[512,256]{1,0:T(8,128)S(1)} %convolution_bitcast_fusion), channel_id=1, source_target_pairs={{0,1},{1,2},{2,3},{3,4},{4,5},{5,6},{6,7},{7,8},{8,9},{9,10},{10,1... | collective-permute-start | bytes 1572872 | tf_op jit(solution)/shard_map/ppermute | solution.py:17
  50.8 1.5 collective-permute-start.4
  52.3 1.0 convolution_bitcast_fusion.2
  53.3 1.3 collective-permute-done.4
  54.6 1.2 maximum_multiply_fusion
  55.9 0.2 convolution_bitcast_fusion.6
  56.0 0.8 copy.28
  56.8 0.0 all-reduce.4.cloned.1.call-update
  56.8 0.6 copy-done.10
  57.5 0.6 dynamic-slice
  58.1 0.1 copy-done.9
  58.1 0.6 dynamic-slice.2
  60.1 112.2 %all-reduce.4.cloned.1.call-done = f32[64,256]{0,1:T(8,128)} async-done(((f32[64,256]{0,1:T(8,128)}), f32[64,256]{0,1:T(8,128)}) %all-reduce.4.cloned.1.call-update) | async-done | bytes 65552
  172.4 1.0 constant_dynamic-slice_fusion
  173.4 3.7 %all-reduce.1 = f32[4,256]{0,1:T(8,128)S(1)} all-reduce(f32[4,256]{0,1:T(8,128)S(1)} %constant_dynamic-slice_fusion), channel_id=3, replica_groups=mesh['wide'=16,'narrow'=2] {'narrow'}, use_global_device_ids=true, to_apply=%region_2.0.clone | all-reduce | flops 1024 | bytes 8192
  177.1 1.0 fusion.15
  (23 shorter events, 0.1 us)
Async XLA Ops:
  7.2 1.5 copy-start
  7.2 7.6 %copy-start.3 = (f32[512,256]{1,0:T(8,128)S(1)}, f32[512,256]{1,0:T(8,128)}, u32[]{:S(2)}) copy-start(f32[512,256]{1,0:T(8,128)} %param.8) | copy-start | bytes 1572868
  7.2 7.4 %copy-start.8 = (f32[16]{0:T(128)S(1)}, f32[16]{0:T(128)}, u32[]{:S(2)}) copy-start(f32[16]{0:T(128)} %param.12) | copy-start | bytes 196
  7.2 7.4 %copy-start.7 = (s32[256]{0:T(256)S(1)}, s32[256]{0:T(256)}, u32[]{:S(2)}) copy-start(s32[256]{0:T(256)} %param.13) | copy-start | bytes 3076
  7.2 7.5 %copy-start.1 = (f32[512,512]{1,0:T(8,128)S(1)}, f32[512,512]{1,0:T(8,128)}, u32[]{:S(2)}) copy-start(f32[512,512]{1,0:T(8,128)} %param.10) | copy-start | bytes 3145732
  7.2 165.1 %all-reduce.4.cloned.1.call-start = ((), (), s32[]{:S(2)}) async-start(), calls=%async_computation | async-start | bytes 262144
  7.3 8.9 %collective-permute-start = (f32[512,256]{1,0:T(8,128)}, f32[512,256]{1,0:T(8,128)S(1)}, u32[]{:S(2)}, u32[]{:S(2)}) collective-permute-start(f32[512,256]{1,0:T(8,128)} %param.8), channel_id=1, source_target_pairs={{1,0},{2,1},{3,2},{4,3},{5,4},{6,5},{7,6},{8,7},{9,8},{10,9},{11,1... | collective-permute-start | bytes 1572872 | tf_op jit(solution)/shard_map/ppermute | solution.py:17
  11.6 4.6 %collective-permute-start.1 = (f32[512,256]{1,0:T(8,128)S(1)}, f32[512,256]{1,0:T(8,128)S(1)}, u32[]{:S(2)}, u32[]{:S(2)}) collective-permute-start(f32[512,256]{1,0:T(8,128)S(1)} %fusion.20), channel_id=1, source_target_pairs={{0,1},{1,2},{2,3},{3,4},{4,5},{5,6},{6,7},{7,8},{8,9},{9,10},{10,1... | collective-permute-start | bytes 1572872 | tf_op jit(solution)/shard_map/ppermute | solution.py:17
  14.8 1.4 copy-start.2
  19.2 14.3 %collective-permute-start.3 = (f32[512,256]{1,0:T(8,128)S(1)}, f32[512,256]{1,0:T(8,128)S(1)}, u32[]{:S(2)}, u32[]{:S(2)}) collective-permute-start(f32[512,256]{1,0:T(8,128)S(1)} %convolution_bitcast_fusion.3), channel_id=1, source_target_pairs={{0,1},{1,2},{2,3},{3,4},{4,5},{5,6},{6,7},{7,8},{8,9},{9,10},{10,1... | collective-permute-start | bytes 1572872 | tf_op jit(solution)/shard_map/ppermute | solution.py:17
  31.1 5.8 %collective-permute-start.2 = (f32[512,256]{1,0:T(8,128)S(1)}, f32[512,256]{1,0:T(8,128)S(1)}, u32[]{:S(2)}, u32[]{:S(2)}) collective-permute-start(f32[512,256]{1,0:T(8,128)S(1)} %maximum_multiply_fusion.2), channel_id=1, source_target_pairs={{1,0},{2,1},{3,2},{4,3},{5,4},{6,5},{7,6},{8,7},{9,8},{10,9},{11,1... | collective-permute-start | bytes 1572872 | tf_op jit(solution)/shard_map/ppermute | solution.py:17
  40.0 13.4 %collective-permute-start.5 = (f32[512,256]{1,0:T(8,128)S(1)}, f32[512,256]{1,0:T(8,128)S(1)}, u32[]{:S(2)}, u32[]{:S(2)}) collective-permute-start(f32[512,256]{1,0:T(8,128)S(1)} %convolution_bitcast_fusion), channel_id=1, source_target_pairs={{0,1},{1,2},{2,3},{3,4},{4,5},{5,6},{6,7},{7,8},{8,9},{9,10},{10,1... | collective-permute-start | bytes 1572872 | tf_op jit(solution)/shard_map/ppermute | solution.py:17
  50.8 3.8 %collective-permute-start.4 = (f32[512,256]{1,0:T(8,128)S(1)}, f32[512,256]{1,0:T(8,128)S(1)}, u32[]{:S(2)}, u32[]{:S(2)}) collective-permute-start(f32[512,256]{1,0:T(8,128)S(1)} %maximum_multiply_fusion.1), channel_id=1, source_target_pairs={{1,0},{2,1},{3,2},{4,3},{5,4},{6,5},{7,6},{8,7},{9,8},{10,9},{11,1... | collective-permute-start | bytes 1572872 | tf_op jit(solution)/shard_map/ppermute | solution.py:17
  53.3 2.5 %copy-start.6 = (bf16[64,512]{1,0:T(8,128)(2,1)S(1)}, bf16[64,512]{1,0:T(8,128)(2,1)}, u32[]{:S(2)}) copy-start(bf16[64,512]{1,0:T(8,128)(2,1)} %param.14) | copy-start | bytes 196612
  55.9 117.5 %copy-start.4 = (f32[512,256]{1,0:T(8,128)}, f32[512,256]{1,0:T(8,128)S(1)}, u32[]{:S(2)}) copy-start(f32[512,256]{1,0:T(8,128)S(1)} %maximum_multiply_fusion) | copy-start | bytes 1572868
  56.8 0.7 copy-start.10
  57.5 0.7 copy-start.9
  60.1 117.0 %copy-start.5 = (f32[256,256]{1,0:T(8,128)S(1)}, f32[256,256]{1,0:T(8,128)}, u32[]{:S(2)}) copy-start(f32[256,256]{1,0:T(8,128)} %param.15) | copy-start | bytes 786436
Sparse Core Ops, SparseCore 0:
  56.9 115.3 all-reduce.3
where the time goes:
time: 185 us
  waiting for transfers between devices  117 us (63%)
  starting transfers between devices  30.1 us (16%)
  between operations  15.6 us (8%)
  matrix products  14.3 us (8%)
  local copies, waits for them, and re-layouts  3.75 us (2%)
  blocking collectives  3.75 us (2%)
    unnamed x2, waiting for transfers between devices  112 us
    ppermute x6, starting transfers between devices, passed_along(): return lax.ppermute(block, axis, route)  30.1 us
    dot_general x7, matrix products, full_dot(): jnp.dot(left, right, precision=lax.Precision.HIGHEST, preferred_element_t...  7.66 us
    dot_general x3, matrix products, transposed_dot(): lax.dot_general(left, right, (((0,), (0,)), ((), ())), precision=lax.Prec...  6.48 us
    ppermute x6, waiting for transfers between devices, passed_along(): return lax.ppermute(block, axis, route)  5.07 us
    unnamed x1, blocking collectives  3.75 us
  transfers between devices with their start and end apart: 7, of which 4 were waited for; matrix products, arithmetic and copies ran while one was open for 4% of the time, Pallas kernels for 0%

commit v1 on v0

v1 whole, which is shorter than its diff:
```python
import functools
import math

import jax
import jax.numpy as jnp
from jax import lax
from jax.experimental import pallas as pl
from jax.experimental.pallas import tpu as pltpu
from jax.sharding import PartitionSpec as P

ITERS = 3
LANES = 128
MESH = pl.DeviceIdType.MESH

step_size = 0.5


def split(value):
    high = value.astype(jnp.bfloat16)
    low = (value - high.astype(jnp.float32)).astype(jnp.bfloat16)
    return high, low


def rows_of(index, size):
    return pl.ds(pl.multiple_of(index * size, size), size)


def kernel(
    n,
    narrow,
    group,
    shrink,
    start_ref,
    marginal_ref,
    diag_ref,
    upper_ref,
    grid_ref,
    index_ref,
    dosages_ref,
    weights_ref,
    effects_ref,
    stacked_ref,
    diag,
    upper,
    marginal,
    dosages,
    weights,
    index,
    grid,
    diag_high,
    diag_low,
    upper_high,
    upper_low,
    turned_high,
    turned_low,
    effects,
    pair,
    ahead_pair,
    base,
    handed,
    ahead,
    behind,
    threshold,
    strip_scores,
    parts,
    part_sum,
    owned,
    load_sem,
    out_sem,
    ahead_send,
    ahead_recv,
    behind_send,
    behind_recv,
    part_send,
    part_recv,
    owned_send,
    owned_recv,
):
    strip, width = start_ref.shape
    halves = width // LANES
    per_owner = stacked_ref.shape[0]
    groups = n // group
    block = min(256, strip)
    blocks = strip // block
    levels = grid_ref.shape[1]

    me = lax.axis_index("wide") * narrow + lax.axis_index("narrow")
    place = lax.rem(me, group)
    team = me // group
    has_prev = me > 0
    has_next = me < n - 1

    def device(i):
        return (i // narrow, lax.rem(i, narrow))

    prev = device(jnp.maximum(me - 1, 0))
    following = device(jnp.minimum(me + 1, n - 1))

    def mate(distance):
        return team * group + lax.rem(place + distance, group)

    def peer(distance):
        return lax.rem(team + distance, groups) * group + place

    barrier = pltpu.get_barrier_semaphore()

    def greet(where):
        pl.semaphore_signal(barrier, inc=1, device_id=where, device_id_type=MESH)

    greet(device(lax.rem(me + n - 1, n)))
    greet(device(lax.rem(me + 1, n)))
    for distance in range(1, group):
        greet(device(mate(distance)))
    for distance in range(1, groups):
        greet(device(peer(distance)))

    loads = []

    def load(source, target):
        copy = pltpu.make_async_copy(source, target, load_sem.at[len(loads)])
        copy.start()
        loads.append(copy)
        return copy

    def lanes(half):
        return pl.ds(half * LANES, LANES)

    upper_load = load(upper_ref, upper)
    start_loads = [load(start_ref.at[:, lanes(h)], effects.at[0, h]) for h in range(halves)]
    diag_load = load(diag_ref, diag)
    marginal_loads = [load(marginal_ref.at[:, lanes(h)], marginal.at[h]) for h in range(halves)]
    index_load = load(index_ref, index)
    grid_load = load(grid_ref, grid)
    dosages_load = load(dosages_ref, dosages)
    weights_load = load(weights_ref, weights)

    pl.semaphore_wait(barrier, group + groups)

    def effects_copy(sweep, half):
        source = start_ref.at[:, lanes(half)] if sweep == 0 else effects.at[sweep, half]
        return pltpu.make_async_remote_copy(
            src_ref=source,
            dst_ref=ahead.at[sweep, half],
            send_sem=ahead_send.at[sweep, half],
            recv_sem=ahead_recv.at[sweep, half],
            device_id=prev,
            device_id_type=MESH,
        )

    def handed_copy(sweep, half):
        return pltpu.make_async_remote_copy(
            src_ref=handed.at[sweep, half],
            dst_ref=behind.at[sweep, half],
            send_sem=behind_send.at[sweep, half],
            recv_sem=behind_recv.at[sweep, half],
            device_id=following,
            device_id_type=MESH,
        )

    def send_effects(sweep, half):
        @pl.when(has_prev)
        def _():
            effects_copy(sweep, half).start()

    for half in range(halves):
        send_effects(0, half)

    def product(high, low, both, rows):
        wide = jnp.dot(high[rows, :], both[...], preferred_element_type=jnp.float32)
        small = jnp.dot(low[rows, :], both[:, :LANES], preferred_element_type=jnp.float32)
        return wide[:, :LANES] + (wide[:, LANES:] + small)

    def split_effects(value, both, rows):
        high, low = split(value)
        both[rows, :LANES] = high
        both[rows, LANES:] = low

    def each_block(body):
        @pl.loop(0, blocks)
        def _(b):
            body(rows_of(b, block))

    upper_load.wait()

    def turn(rows):
        high, low = split(upper[:, rows].T)
        turned_high[rows, :] = high
        turned_low[rows, :] = low

    for b in range(blocks):
        turn(pl.ds(b * block, block))

    def hand_on(sweep, half):
        @pl.when(has_next)
        def _():
            def body(rows):
                handed[sweep, half, rows, :] = product(turned_high, turned_low, pair.at[half], rows)

            each_block(body)
            handed_copy(sweep, half).start()

    def own_term(sweep, half):
        def body(rows):
            own = product(diag_high, diag_low, pair.at[half], rows)
            gradient = own - marginal[half, rows, :]
            base[half, rows, :] = effects[sweep, half, rows, :] - step_size * gradient

        each_block(body)

    for half in range(halves):
        start_loads[half].wait()

        def body(rows, half=half):
            split_effects(effects[0, half, rows, :], pair.at[half], rows)

        each_block(body)
        hand_on(0, half)

    def split_upper(rows):
        high, low = split(upper[rows, :])
        upper_high[rows, :] = high
        upper_low[rows, :] = low

    each_block(split_upper)
    diag_load.wait()

    def split_diag(rows):
        high, low = split(diag[rows, :])
        diag_high[rows, :] = high
        diag_low[rows, :] = low

    each_block(split_diag)
    for half in range(halves):
        marginal_loads[half].wait()
        own_term(0, half)
    index_load.wait()
    grid_load.wait()
    picked = jnp.zeros((1, width), jnp.float32)
    for level in range(levels):
        picked = jnp.where(index[...] == level, grid[0, level], picked)
    threshold[...] = step_size * picked
    dosages_load.wait()
    weights_load.wait()

    def finish(sweep, half):
        @pl.when(has_next)
        def _():
            effects_copy(sweep, half).wait_recv()

            def body(rows):
                split_effects(ahead[sweep, half, rows, :], ahead_pair, rows)

            each_block(body)

            def add(rows):
                coupled = product(upper_high, upper_low, ahead_pair, rows)
                base[half, rows, :] = base[half, rows, :] - step_size * coupled

            each_block(add)

        @pl.when(has_prev)
        def _():
            handed_copy(sweep, half).wait_recv()

            def add(rows):
                base[half, rows, :] = base[half, rows, :] - step_size * behind[sweep, half, rows, :]

            each_block(add)

        limit = threshold[:, half * LANES : (half + 1) * LANES]

        def shrink_rows(rows):
            moved = base[half, rows, :]
            fresh = moved - jnp.minimum(jnp.maximum(moved, -limit), limit)
            effects[sweep + 1, half, rows, :] = fresh
            split_effects(fresh, pair.at[half], rows)

        each_block(shrink_rows)

    def part_copy(half, distance):
        return pltpu.make_async_remote_copy(
            src_ref=strip_scores.at[half, lax.rem(place + distance, group)],
            dst_ref=parts.at[half, distance],
            send_sem=part_send.at[half, distance],
            recv_sem=part_recv.at[half, distance],
            device_id=device(mate(distance)),
            device_id_type=MESH,
        )

    def owned_copy(half, distance):
        return pltpu.make_async_remote_copy(
            src_ref=part_sum.at[half, lax.rem(team + distance, groups)],
            dst_ref=owned.at[half, distance],
            send_sem=owned_send.at[half, distance],
            recv_sem=owned_recv.at[half, distance],
            device_id=device(peer(distance)),
            device_id_type=MESH,
        )

    out_copies = []

    def score(half):
        copy = pltpu.make_async_copy(
            effects.at[ITERS, half], effects_ref.at[:, lanes(half)], out_sem.at[half]
        )
        copy.start()
        out_copies.append(copy)
        scores = jnp.dot(
            dosages[...], pair[half, :, :LANES], preferred_element_type=jnp.float32
        )
        for t in range(groups):
            for p in range(group):
                at = (t * group + p) * per_owner
                strip_scores[half, p, t * per_owner : (t + 1) * per_owner, :] = scores[
                    at : at + per_owner
                ]
        for distance in range(1, group):
            part_copy(half, distance).start()

    def gather_parts(half):
        total = strip_scores[half, place]
        for distance in range(1, group):
            part_copy(half, distance).wait_recv()
            total = total + parts[half, distance]
        for t in range(groups):
            part_sum[half, t] = total[t * per_owner : (t + 1) * per_owner]
        for distance in range(1, groups):
            owned_copy(half, distance).start()

    def gather_owned(half):
        total = part_sum[half, team]
        for distance in range(1, groups):
            owned_copy(half, distance).wait_recv()
            total = total + owned[half, distance]
        return total * shrink

    for sweep in range(ITERS):
        for half in range(halves):
            finish(sweep, half)
            if sweep + 1 < ITERS:
                send_effects(sweep + 1, half)
                hand_on(sweep + 1, half)
                own_term(sweep + 1, half)
            else:
                score(half)

    for half in range(halves):
        gather_parts(half)
    stacked = None
    for half in range(halves):
        term = jnp.dot(
            gather_owned(half),
            weights[half * LANES : (half + 1) * LANES, :],
            precision=lax.Precision.HIGHEST,
            preferred_element_type=jnp.float32,
        )
        stacked = term if stacked is None else stacked + term
    stacked_ref[...] = stacked

    for copy in out_copies:
        copy.wait()
    for half in range(halves):
        for distance in range(1, group):
            part_copy(half, distance).wait_send()
        for distance in range(1, groups):
            owned_copy(half, distance).wait_send()

    @pl.when(has_prev)
    def _():
        for sweep in range(ITERS):
            for half in range(halves):
                effects_copy(sweep, half).wait_send()

    @pl.when(has_next)
    def _():
        for sweep in range(ITERS):
            for half in range(halves):
                handed_copy(sweep, half).wait_send()


def group_size(n):
    size = 1
    while size * size < n or n % size:
        size += 1
    return size


def solution(mesh):
    wide, narrow = mesh.shape["wide"], mesh.shape["narrow"]
    n = wide * narrow

    def shards(
        effects_start, marginal, ld_diag, ld_upper, penalty_grid, penalty_index, dosages, stack_weights
    ):
        strip, width = effects_start.shape
        halves = width // LANES
        people = dosages.shape[0]
        levels = penalty_grid.shape[0]
        per_owner = people // n
        group = group_size(n)
        groups = n // group
        f32, bf16 = jnp.float32, jnp.bfloat16
        anywhere = pl.BlockSpec(memory_space=pl.ANY)
        dma = pltpu.SemaphoreType.DMA
        call = pl.pallas_call(
            functools.partial(kernel, n, narrow, group, 1.0 / math.sqrt(strip * n)),
            out_shape=(
                jax.ShapeDtypeStruct((strip, width), f32),
                jax.ShapeDtypeStruct((per_owner, width), f32),
            ),
            in_specs=[pl.BlockSpec(memory_space=pltpu.HBM)] * 8,
            out_specs=(anywhere, pl.BlockSpec(memory_space=pltpu.VMEM)),
            scratch_shapes=[
                pltpu.VMEM((strip, strip), f32),
                pltpu.VMEM((strip, strip), f32),
                pltpu.VMEM((halves, strip, LANES), f32),
                pltpu.VMEM((people, strip), bf16),
                pltpu.VMEM((width, width), f32),
                pltpu.VMEM((1, width), jnp.int32),
                pltpu.SMEM((1, levels), f32),
                *[pltpu.VMEM((strip, strip), bf16)] * 6,
                pltpu.VMEM((ITERS + 1, halves, strip, LANES), f32),
                pltpu.VMEM((halves, strip, 2 * LANES), bf16),
                pltpu.VMEM((strip, 2 * LANES), bf16),
                pltpu.VMEM((halves, strip, LANES), f32),
                pltpu.VMEM((ITERS, halves, strip, LANES), f32),
                pltpu.VMEM((ITERS, halves, strip, LANES), f32),
                pltpu.VMEM((ITERS, halves, strip, LANES), f32),
                pltpu.VMEM((1, width), f32),
                pltpu.VMEM((halves, group, groups * per_owner, LANES), f32),
                pltpu.VMEM((halves, group, groups * per_owner, LANES), f32),
                pltpu.VMEM((halves, groups, per_owner, LANES), f32),
                pltpu.VMEM((halves, groups, per_owner, LANES), f32),
                dma((6 + 2 * halves,)),
                dma((halves,)),
                *[dma((ITERS, halves))] * 4,
                *[dma((halves, group))] * 2,
                *[dma((halves, groups))] * 2,
            ],
            compiler_params=pltpu.CompilerParams(
                collective_id=0, has_side_effects=True, vmem_limit_bytes=60 * 2**20
            ),
            cost_estimate=pl.CostEstimate(
                flops=2 * 9 * ITERS * strip * strip * width,
                bytes_accessed=4 * (2 * strip * strip + 3 * strip * width),
                transcendentals=0,
            ),
        )
        return call(
            effects_start,
            marginal,
            ld_diag,
            ld_upper,
            penalty_grid[None, :],
            penalty_index[None, :],
            dosages,
            stack_weights,
        )

    return jax.shard_map(
        shards,
        mesh=mesh,
        in_specs=(
            P(("wide", "narrow"), None),
            P(("wide", "narrow"), None),
            P(("wide", "narrow"), None),
            P(("wide", "narrow"), None),
            P(),
            P(),
            P(None, ("wide", "narrow")),
            P(),
        ),
        out_specs=(P(("wide", "narrow"), None), P(("wide", "narrow"), None)),
        check_vma=False,
    )
```

time: 185 us -> 59.5 us (0.32)
  waiting for transfers between devices: 117 us -> 0 us
  Pallas kernels: 0 us -> 56.2 us
  starting transfers between devices: 30.1 us -> 0 us
  between operations: 15.6 us -> 0.65 us
  matrix products: 14.3 us -> 0 us
  blocking collectives: 3.75 us -> 0 us
    unnamed x2 -> x0, waiting for transfers between devices: 112 us -> none
    pallas_call x0 -> x1, Pallas kernels: none -> 56.2 us  [shards(): call(effects_start, marginal, ld_diag, ld_upper, penalty_grid[None, :], p...]
    ppermute x6 -> x0, starting transfers between devices: 30.1 us -> none  [passed_along(): return lax.ppermute(block, axis, route)]
    dot_general x11 -> x0, matrix products: 14.3 us -> none  [the longest x7 7.66 us: full_dot(): jnp.dot(left, right, precision=lax.Precision.HIGHEST, preferred_element_t...]
    ppermute x6 -> x0, waiting for transfers between devices: 5.07 us -> none  [passed_along(): return lax.ppermute(block, axis, route)]
    unnamed x1 -> x0, blocking collectives: 3.75 us -> none
  transfers between devices with their start and end apart: 7 -> 0, of which waited for: 4 -> 0; matrix products, arithmetic and copies ran while one was open for 4% -> 0% of each run, Pallas kernels for 0% -> 0%
where the time goes in v1:
time: 59.5 us; the launch traced here: 59.3 us
  Pallas kernels  56.2 us (94%)
  local copies, waits for them, and re-layouts  2.45 us (4%)
  between operations  0.65 us (1%)
    pallas_call x1, Pallas kernels, shards(): call(effects_start, marginal, ld_diag, ld_upper, penalty_grid[None, :], p...  56.2 us
    unnamed x4, local copies, waits for them, and re-layouts  2.45 us

profile of v1, /device:TPU:0, one launch (start us, length us, event | category | flops | bytes accessed | tf_op | source)
XLA Modules:
  0.0 59.3 jit_solution(9105674139847257478)
XLA Ops:
  0.6 56.2 %shard_map.95 = (f32[512,256]{1,0:T(8,128)}, f32[2,256]{1,0:T(2,128)}) custom-call(f32[512,256]{1,0:T(8,128)} %start_ref.1, f32[512,256]{1,0:T(8,128)} %marginal_ref.1, f32[512,512]{1,0:T(8,128)} %diag_ref.1, f32[512,512]{1,0:T(8,128)} %upper_ref.1, f32[1,16]{1,0:T(1,128)} %bitcast.3, s32[1,256]{1,0:T(1,128)} %bitcast.2, bf16[64,512]{1,0:T(8,128)(2,1)} %dosages_ref.1, ...), custom_call_target="tpu_custom_call" | custom-call | flops 3623878656 | bytes 3670016 | tf_op jit(solution)/shard_map/pallas_call | solution.py:449
  56.9 0.0 copy-start
  56.9 1.9 %copy.12 = f32[512,256]{1,0:T(8,128)} copy(f32[512,256]{1,0:T(8,128)} %get-tuple-element.4) | data formatting | bytes 1048576
  58.8 0.0 copy-done
  58.8 0.6 copy.13
Async XLA Ops:
  56.9 1.9 %copy-start = (f32[2,256]{1,0:T(2,128)S(1)}, f32[2,256]{1,0:T(2,128)}, u32[]{:S(2)}) copy-start(f32[2,256]{1,0:T(2,128)} %get-tuple-element.5) | copy-start | bytes 6148

commit v2 on v1

--- a/solution.py
+++ b/solution.py
@@ -19,6 +19,10 @@
     high = value.astype(jnp.bfloat16)
     low = (value - high.astype(jnp.float32)).astype(jnp.bfloat16)
     return high, low
+
+
+def shrunk(moved, limit):
+    return moved - jnp.minimum(jnp.maximum(moved, -limit), limit)
 
 
 def rows_of(index, size):
@@ -38,7 +42,8 @@
     index_ref,
     dosages_ref,
     weights_ref,
-    effects_ref,
+    moved_ref,
+    threshold,
     stacked_ref,
     diag,
     upper,
@@ -60,7 +65,6 @@
     handed,
     ahead,
     behind,
-    threshold,
     strip_scores,
     parts,
     part_sum,
@@ -80,7 +84,7 @@
     halves = width // LANES
     per_owner = stacked_ref.shape[0]
     groups = n // group
-    block = min(256, strip)
+    block = row_block(strip)
     blocks = strip // block
     levels = grid_ref.shape[1]
 
@@ -136,34 +140,40 @@
 
     pl.semaphore_wait(barrier, group + groups)
 
-    def effects_copy(sweep, half):
-        source = start_ref.at[:, lanes(half)] if sweep == 0 else effects.at[sweep, half]
+    def block_rows(b):
+        return pl.ds(b * block, block)
+
+    def effects_copy(sweep, half, b):
+        rows = block_rows(b)
+        source = start_ref.at[rows, lanes(half)] if sweep == 0 else effects.at[sweep, half, rows]
         return pltpu.make_async_remote_copy(
             src_ref=source,
-            dst_ref=ahead.at[sweep, half],
-            send_sem=ahead_send.at[sweep, half],
-            recv_sem=ahead_recv.at[sweep, half],
+            dst_ref=ahead.at[sweep, half, rows],
+            send_sem=ahead_send.at[sweep, half, b],
+            recv_sem=ahead_recv.at[sweep, half, b],
             device_id=prev,
             device_id_type=MESH,
         )
 
-    def handed_copy(sweep, half):
+    def handed_copy(sweep, half, b):
+        rows = block_rows(b)
         return pltpu.make_async_remote_copy(
-            src_ref=handed.at[sweep, half],
-            dst_ref=behind.at[sweep, half],
-            send_sem=behind_send.at[sweep, half],
-            recv_sem=behind_recv.at[sweep, half],
+            src_ref=handed.at[sweep, half, rows],
+            dst_ref=behind.at[sweep, half, rows],
+            send_sem=behind_send.at[sweep, half, b],
+            recv_sem=behind_recv.at[sweep, half, b],
             device_id=following,
             device_id_type=MESH,
         )
 
-    def send_effects(sweep, half):
+    def send_effects(sweep, half, b):
         @pl.when(has_prev)
         def _():
-            effects_copy(sweep, half).start()
+            effects_copy(sweep, half, b).start()
 
     for half in range(halves):
-        send_effects(0, half)
+        for b in range(blocks):
+            send_effects(0, half, b)
 
     def product(high, low, both, rows):
         wide = jnp.dot(high[rows, :], both[...], preferred_element_type=jnp.float32)
@@ -193,11 +203,10 @@
     def hand_on(sweep, half):
         @pl.when(has_next)
         def _():
-            def body(rows):
+            for b in range(blocks):
+                rows = block_rows(b)
                 handed[sweep, half, rows, :] = product(turned_high, turned_low, pair.at[half], rows)
-
-            each_block(body)
-            handed_copy(sweep, half).start()
+                handed_copy(sweep, half, b).start()
 
     def own_term(sweep, half):
         def body(rows):
@@ -232,50 +241,60 @@
     each_block(split_diag)
     for half in range(halves):
         marginal_loads[half].wait()
-        own_term(0, half)
     index_load.wait()
     grid_load.wait()
     picked = jnp.zeros((1, width), jnp.float32)
     for level in range(levels):
         picked = jnp.where(index[...] == level, grid[0, level], picked)
     threshold[...] = step_size * picked
+
+    @pl.when(me == n - 1)
+    def _():
+        ahead[...] = jnp.zeros_like(ahead)
+
+    @pl.when(me == 0)
+    def _():
+        behind[...] = jnp.zeros_like(behind)
+
     dosages_load.wait()
     weights_load.wait()
 
+    out_copies = []
+
     def finish(sweep, half):
-        @pl.when(has_next)
-        def _():
-            effects_copy(sweep, half).wait_recv()
-
-            def body(rows):
-                split_effects(ahead[sweep, half, rows, :], ahead_pair, rows)
-
-            each_block(body)
-
-            def add(rows):
-                coupled = product(upper_high, upper_low, ahead_pair, rows)
-                base[half, rows, :] = base[half, rows, :] - step_size * coupled
-
-            each_block(add)
-
-        @pl.when(has_prev)
-        def _():
-            handed_copy(sweep, half).wait_recv()
-
-            def add(rows):
-                base[half, rows, :] = base[half, rows, :] - step_size * behind[sweep, half, rows, :]
-
-            each_block(add)
+        last = sweep + 1 == ITERS
+        for b in range(blocks):
+
+            @pl.when(has_next)
+            def _(b=b):
+                effects_copy(sweep, half, b).wait_recv()
+
+            rows = block_rows(b)
+            split_effects(ahead[sweep, half, rows, :], ahead_pair, rows)
 
         limit = threshold[:, half * LANES : (half + 1) * LANES]
-
-        def shrink_rows(rows):
-            moved = base[half, rows, :]
-            fresh = moved - jnp.minimum(jnp.maximum(moved, -limit), limit)
-            effects[sweep + 1, half, rows, :] = fresh
+        for b in range(blocks):
+            rows = block_rows(b)
+            coupled = product(upper_high, upper_low, ahead_pair, rows)
+
+            @pl.when(has_prev)
+            def _(b=b):
+                handed_copy(sweep, half, b).wait_recv()
+
+            moved = base[half, rows, :] - step_size * (coupled + behind[sweep, half, rows, :])
+            fresh = shrunk(moved, limit)
             split_effects(fresh, pair.at[half], rows)
-
-        each_block(shrink_rows)
+            if last:
+                base[half, rows, :] = moved
+            else:
+                effects[sweep + 1, half, rows, :] = fresh
+                send_effects(sweep + 1, half, b)
+        if last:
+            copy = pltpu.make_async_copy(
+                base.at[half], moved_ref.at[:, lanes(half)], out_sem.at[half]
+            )
+            copy.start()
+            out_copies.append(copy)
 
     def part_copy(half, distance):
         return pltpu.make_async_remote_copy(
@@ -297,14 +316,7 @@
             device_id_type=MESH,
         )
 
-    out_copies = []
-
     def score(half):
-        copy = pltpu.make_async_copy(
-            effects.at[ITERS, half], effects_ref.at[:, lanes(half)], out_sem.at[half]
-        )
-        copy.start()
-        out_copies.append(copy)
         scores = jnp.dot(
             dosages[...], pair[half, :, :LANES], preferred_element_type=jnp.float32
         )
@@ -336,16 +348,15 @@
 
     for sweep in range(ITERS):
         for half in range(halves):
+            own_term(sweep, half)
             finish(sweep, half)
             if sweep + 1 < ITERS:
-                send_effects(sweep + 1, half)
                 hand_on(sweep + 1, half)
-                own_term(sweep + 1, half)
             else:
                 score(half)
-
-    for half in range(halves):
-        gather_parts(half)
+                if half > 0:
+                    gather_parts(half - 1)
+    gather_parts(halves - 1)
     stacked = None
     for half in range(halves):
         term = jnp.dot(
@@ -369,13 +380,19 @@
     def _():
         for sweep in range(ITERS):
             for half in range(halves):
-                effects_copy(sweep, half).wait_send()
+                for b in range(blocks):
+                    effects_copy(sweep, half, b).wait_send()
 
     @pl.when(has_next)
     def _():
         for sweep in range(ITERS):
             for half in range(halves):
-                handed_copy(sweep, half).wait_send()
+                for b in range(blocks):
+                    handed_copy(sweep, half, b).wait_send()
+
+
+def row_block(strip):
+    return min(256, strip)
 
 
 def group_size(n):
@@ -406,10 +423,11 @@
             functools.partial(kernel, n, narrow, group, 1.0 / math.sqrt(strip * n)),
             out_shape=(
                 jax.ShapeDtypeStruct((strip, width), f32),
+                jax.ShapeDtypeStruct((1, width), f32),
                 jax.ShapeDtypeStruct((per_owner, width), f32),
             ),
             in_specs=[pl.BlockSpec(memory_space=pltpu.HBM)] * 8,
-            out_specs=(anywhere, pl.BlockSpec(memory_space=pltpu.VMEM)),
+            out_specs=(anywhere, *[pl.BlockSpec(memory_space=pltpu.VMEM)] * 2),
             scratch_shapes=[
                 pltpu.VMEM((strip, strip), f32),
                 pltpu.VMEM((strip, strip), f32),
@@ -419,21 +437,20 @@
                 pltpu.VMEM((1, width), jnp.int32),
                 pltpu.SMEM((1, levels), f32),
                 *[pltpu.VMEM((strip, strip), bf16)] * 6,
-                pltpu.VMEM((ITERS + 1, halves, strip, LANES), f32),
+                pltpu.VMEM((ITERS, halves, strip, LANES), f32),
                 pltpu.VMEM((halves, strip, 2 * LANES), bf16),
                 pltpu.VMEM((strip, 2 * LANES), bf16),
                 pltpu.VMEM((halves, strip, LANES), f32),
                 pltpu.VMEM((ITERS, halves, strip, LANES), f32),
                 pltpu.VMEM((ITERS, halves, strip, LANES), f32),
                 pltpu.VMEM((ITERS, halves, strip, LANES), f32),
-                pltpu.VMEM((1, width), f32),
                 pltpu.VMEM((halves, group, groups * per_owner, LANES), f32),
                 pltpu.VMEM((halves, group, groups * per_owner, LANES), f32),
                 pltpu.VMEM((halves, groups, per_owner, LANES), f32),
                 pltpu.VMEM((halves, groups, per_owner, LANES), f32),
                 dma((6 + 2 * halves,)),
                 dma((halves,)),
-                *[dma((ITERS, halves))] * 4,
+                *[dma((ITERS, halves, strip // row_block(strip)))] * 4,
                 *[dma((halves, group))] * 2,
                 *[dma((halves, groups))] * 2,
             ],
@@ -446,7 +463,7 @@
                 transcendentals=0,
             ),
         )
-        return call(
+        moved, threshold, stacked = call(
             effects_start,
             marginal,
             ld_diag,
@@ -456,6 +473,7 @@
             dosages,
             stack_weights,
         )
+        return shrunk(moved, threshold), stacked
 
     return jax.shard_map(
         shards,

time: 59.5 us -> 59.9 us (level)
  other arithmetic: 0 us -> 1.9 us
  local copies, waits for them, and re-layouts: 2.45 us -> 1.24 us
    sub x0 -> x1, other arithmetic: none -> 1.89 us  [shrunk(): return moved - jnp.minimum(jnp.maximum(moved, -limit), limit)]
    unnamed x4 -> x5, local copies, waits for them, and re-layouts: 2.45 us -> 1.24 us
where the time goes in v2:
time: 59.9 us; the launch traced here: 59.8 us
  Pallas kernels  56 us (93%)
  other arithmetic  1.9 us (3%)
  local copies, waits for them, and re-layouts  1.24 us (2%)
  between operations  0.65 us (1%)
    pallas_call x1, Pallas kernels, shards(): call(effects_start, marginal, ld_diag, ld_upper, penalty_grid[None, :], p...  56 us
    sub x1, other arithmetic, shrunk(): return moved - jnp.minimum(jnp.maximum(moved, -limit), limit)  1.89 us
    unnamed x5, local copies, waits for them, and re-layouts  1.24 us

profile of v2, /device:TPU:0, one launch (start us, length us, event | category | flops | bytes accessed | tf_op | source)
XLA Modules:
  0.0 59.8 jit_solution(4523444983417137178)
XLA Ops:
  0.6 56.0 %shard_map.95 = (f32[512,256]{1,0:T(8,128)}, f32[1,256]{1,0:T(1,128)}, f32[2,256]{1,0:T(2,128)}) custom-call(f32[512,256]{1,0:T(8,128)} %start_ref.1, f32[512,256]{1,0:T(8,128)} %marginal_ref.1, f32[512,512]{1,0:T(8,128)} %diag_ref.1, f32[512,512]{1,0:T(8,128)} %upper_ref.1, f32[1,16]{1,0:T(1,128)} %bitcast.7, s32[1,256]{1,0:T(1,128)} %bitcast.6, ...), custom_call_target="tpu_custom_call" | custom-call | flops 3623878656 | bytes 3670016 | tf_op jit(solution)/shard_map/pallas_call | solution.py:466
  56.6 0.0 copy-start
  56.6 0.7 %copy-done = f32[1,256]{1,0:T(1,128)S(1)} copy-done((f32[1,256]{1,0:T(1,128)S(1)}, f32[1,256]{1,0:T(1,128)}, u32[]{:S(2)}) %copy-start) | copy-done | bytes 1048
  57.3 0.0 copy-start.1
  57.3 1.9 %minimum_subtract_fusion = f32[512,256]{1,0:T(8,128)} fusion(f32[512,256]{1,0:T(8,128)} %get-tuple-element.5, f32[256]{0:T(256)S(1)} %bitcast.4, f32[256]{0:T(256)S(1)} %bitcast.5), kind=kLoop, calls=%fused_computation | loop fusion | flops 393216 | bytes 1050624 | tf_op jit(solution)/shard_map/sub | solution.py:25
  59.2 0.0 copy-done.1
  59.2 0.6 copy.11
  (1 shorter events, 0.0 us)
Async XLA Ops:
  56.6 0.7 %copy-start = (f32[1,256]{1,0:T(1,128)S(1)}, f32[1,256]{1,0:T(1,128)}, u32[]{:S(2)}) copy-start(f32[1,256]{1,0:T(1,128)} %get-tuple-element.6) | copy-start | bytes 3076
  57.3 1.9 %copy-start.1 = (f32[2,256]{1,0:T(2,128)S(1)}, f32[2,256]{1,0:T(2,128)}, u32[]{:S(2)}) copy-start(f32[2,256]{1,0:T(2,128)} %get-tuple-element.11) | copy-start | bytes 6148

commit v3 on v2

--- a/solution.py
+++ b/solution.py
@@ -42,8 +42,7 @@
     index_ref,
     dosages_ref,
     weights_ref,
-    moved_ref,
-    threshold,
+    effects_ref,
     stacked_ref,
     diag,
     upper,
@@ -65,6 +64,7 @@
     handed,
     ahead,
     behind,
+    threshold,
     strip_scores,
     parts,
     part_sum,
@@ -171,9 +171,8 @@
         def _():
             effects_copy(sweep, half, b).start()
 
-    for half in range(halves):
-        for b in range(blocks):
-            send_effects(0, half, b)
+    for b in range(blocks):
+        send_effects(0, 0, b)
 
     def product(high, low, both, rows):
         wide = jnp.dot(high[rows, :], both[...], preferred_element_type=jnp.float32)
@@ -200,13 +199,14 @@
     for b in range(blocks):
         turn(pl.ds(b * block, block))
 
-    def hand_on(sweep, half):
+    def hand_on(sweep, half, sent=True):
         @pl.when(has_next)
         def _():
             for b in range(blocks):
                 rows = block_rows(b)
                 handed[sweep, half, rows, :] = product(turned_high, turned_low, pair.at[half], rows)
-                handed_copy(sweep, half, b).start()
+                if sent:
+                    handed_copy(sweep, half, b).start()
 
     def own_term(sweep, half):
         def body(rows):
@@ -223,7 +223,7 @@
             split_effects(effects[0, half, rows, :], pair.at[half], rows)
 
         each_block(body)
-        hand_on(0, half)
+        hand_on(0, half, sent=half == 0)
 
     def split_upper(rows):
         high, low = split(upper[rows, :])
@@ -259,6 +259,15 @@
     dosages_load.wait()
     weights_load.wait()
 
+    for half in range(1, halves):
+
+        @pl.when(has_next)
+        def _(half=half):
+            for b in range(blocks):
+                handed_copy(0, half - 1, b).wait_send()
+                handed_copy(0, half, b).start()
+
+
     out_copies = []
 
     def finish(sweep, half):
@@ -271,27 +280,40 @@
 
             rows = block_rows(b)
             split_effects(ahead[sweep, half, rows, :], ahead_pair, rows)
+
+        first = sweep == 0 and half + 1 < halves
+        if first:
+
+            @pl.when(has_prev)
+            def _():
+                for b in range(blocks):
+                    handed_copy(sweep, half, b).wait_recv()
+                for b in range(blocks):
+                    effects_copy(sweep, half, b).wait_send()
+                    effects_copy(sweep, half + 1, b).start()
 
         limit = threshold[:, half * LANES : (half + 1) * LANES]
         for b in range(blocks):
             rows = block_rows(b)
             coupled = product(upper_high, upper_low, ahead_pair, rows)
 
-            @pl.when(has_prev)
-            def _(b=b):
-                handed_copy(sweep, half, b).wait_recv()
+            if not first:
+
+                @pl.when(has_prev)
+                def _(b=b):
+                    handed_copy(sweep, half, b).wait_recv()
 
             moved = base[half, rows, :] - step_size * (coupled + behind[sweep, half, rows, :])
             fresh = shrunk(moved, limit)
             split_effects(fresh, pair.at[half], rows)
             if last:
-                base[half, rows, :] = moved
+                base[half, rows, :] = fresh
             else:
                 effects[sweep + 1, half, rows, :] = fresh
                 send_effects(sweep + 1, half, b)
         if last:
             copy = pltpu.make_async_copy(
-                base.at[half], moved_ref.at[:, lanes(half)], out_sem.at[half]
+                base.at[half], effects_ref.at[:, lanes(half)], out_sem.at[half]
             )
             copy.start()
             out_copies.append(copy)
@@ -380,6 +402,8 @@
     def _():
         for sweep in range(ITERS):
             for half in range(halves):
+                if sweep == 0 and half + 1 < halves:
+                    continue
                 for b in range(blocks):
                     effects_copy(sweep, half, b).wait_send()
 
@@ -387,6 +411,8 @@
     def _():
         for sweep in range(ITERS):
             for half in range(halves):
+                if sweep == 0 and half + 1 < halves:
+                    continue
                 for b in range(blocks):
                     handed_copy(sweep, half, b).wait_send()
 
@@ -423,11 +449,10 @@
             functools.partial(kernel, n, narrow, group, 1.0 / math.sqrt(strip * n)),
             out_shape=(
                 jax.ShapeDtypeStruct((strip, width), f32),
-                jax.ShapeDtypeStruct((1, width), f32),
                 jax.ShapeDtypeStruct((per_owner, width), f32),
             ),
             in_specs=[pl.BlockSpec(memory_space=pltpu.HBM)] * 8,
-            out_specs=(anywhere, *[pl.BlockSpec(memory_space=pltpu.VMEM)] * 2),
+            out_specs=(anywhere, pl.BlockSpec(memory_space=pltpu.VMEM)),
             scratch_shapes=[
                 pltpu.VMEM((strip, strip), f32),
                 pltpu.VMEM((strip, strip), f32),
@@ -444,6 +469,7 @@
                 pltpu.VMEM((ITERS, halves, strip, LANES), f32),
                 pltpu.VMEM((ITERS, halves, strip, LANES), f32),
                 pltpu.VMEM((ITERS, halves, strip, LANES), f32),
+                pltpu.VMEM((1, width), f32),
                 pltpu.VMEM((halves, group, groups * per_owner, LANES), f32),
                 pltpu.VMEM((halves, group, groups * per_owner, LANES), f32),
                 pltpu.VMEM((halves, groups, per_owner, LANES), f32),
@@ -463,7 +489,7 @@
                 transcendentals=0,
             ),
         )
-        moved, threshold, stacked = call(
+        return call(
             effects_start,
             marginal,
             ld_diag,
@@ -473,8 +499,6 @@
             dosages,
             stack_weights,
         )
-        return shrunk(moved, threshold), stacked
-
     return jax.shard_map(
         shards,
         mesh=mesh,

time: 59.9 us -> 56.6 us (0.945)
  Pallas kernels: 56 us -> 53.3 us
  other arithmetic: 1.9 us -> 0 us
  local copies, waits for them, and re-layouts: 1.24 us -> 2.45 us
    pallas_call x1, Pallas kernels: 56 us -> 53.3 us  [shards(): call(effects_start, marginal, ld_diag, ld_upper, penalty_grid[None, :], p...]
    sub x1 -> x0, other arithmetic: 1.89 us -> none  [shrunk(): return moved - jnp.minimum(jnp.maximum(moved, -limit), limit)]
    unnamed x5 -> x4, local copies, waits for them, and re-layouts: 1.24 us -> 2.45 us
where the time goes in v3:
time: 56.6 us; the launch traced here: 56.4 us
  Pallas kernels  53.3 us (94%)
  local copies, waits for them, and re-layouts  2.45 us (4%)
  between operations  0.65 us (1%)
    pallas_call x1, Pallas kernels, shards(): call(effects_start, marginal, ld_diag, ld_upper, penalty_grid[None, :], p...  53.3 us
    unnamed x4, local copies, waits for them, and re-layouts  2.45 us

profile of v3, /device:TPU:0, one launch (start us, length us, event | category | flops | bytes accessed | tf_op | source)
XLA Modules:
  0.0 56.4 jit_solution(40951904313552413)
XLA Ops:
  0.6 53.3 %shard_map.95 = (f32[512,256]{1,0:T(8,128)}, f32[2,256]{1,0:T(2,128)}) custom-call(f32[512,256]{1,0:T(8,128)} %start_ref.1, f32[512,256]{1,0:T(8,128)} %marginal_ref.1, f32[512,512]{1,0:T(8,128)} %diag_ref.1, f32[512,512]{1,0:T(8,128)} %upper_ref.1, f32[1,16]{1,0:T(1,128)} %bitcast.3, s32[1,256]{1,0:T(1,128)} %bitcast.2, bf16[64,512]{1,0:T(8,128)(2,1)} %dosages_ref.1, ...), custom_call_target="tpu_custom_call" | custom-call | flops 3623878656 | bytes 3670016 | tf_op jit(solution)/shard_map/pallas_call | solution.py:492
  54.0 0.0 copy-start
  54.0 1.9 %copy.12 = f32[512,256]{1,0:T(8,128)} copy(f32[512,256]{1,0:T(8,128)} %get-tuple-element.4) | data formatting | bytes 1048576
  55.9 0.0 copy-done
  55.9 0.6 %copy.13 = f32[2,256]{1,0:T(2,128)} copy(f32[2,256]{1,0:T(2,128)S(1)} %copy-done) | data formatting | bytes 4096
Async XLA Ops:
  54.0 1.9 %copy-start = (f32[2,256]{1,0:T(2,128)S(1)}, f32[2,256]{1,0:T(2,128)}, u32[]{:S(2)}) copy-start(f32[2,256]{1,0:T(2,128)} %get-tuple-element.5) | copy-start | bytes 6148

commit v4 on v3

--- a/solution.py
+++ b/solution.py
@@ -368,25 +368,29 @@
             total = total + owned[half, distance]
         return total * shrink
 
+    def stack(half):
+        return jnp.dot(
+            gather_owned(half),
+            weights[half * LANES : (half + 1) * LANES, :],
+            precision=lax.Precision.HIGHEST,
+            preferred_element_type=jnp.float32,
+        )
+
     for sweep in range(ITERS):
         for half in range(halves):
             own_term(sweep, half)
+            if sweep + 1 == ITERS and half > 0:
+                gather_parts(half - 1)
             finish(sweep, half)
             if sweep + 1 < ITERS:
                 hand_on(sweep + 1, half)
             else:
                 score(half)
-                if half > 0:
-                    gather_parts(half - 1)
-    gather_parts(halves - 1)
     stacked = None
     for half in range(halves):
-        term = jnp.dot(
-            gather_owned(half),
-            weights[half * LANES : (half + 1) * LANES, :],
-            precision=lax.Precision.HIGHEST,
-            preferred_element_type=jnp.float32,
-        )
+        if half + 1 == halves:
+            gather_parts(half)
+        term = stack(half)
         stacked = term if stacked is None else stacked + term
     stacked_ref[...] = stacked
 
@@ -415,6 +419,21 @@
                     continue
                 for b in range(blocks):
                     handed_copy(sweep, half, b).wait_send()
+
+
+def hand_out(effects_ref, stacked_ref, effects_out, stacked_out, sems):
+    pieces = sems.shape[0] - 1
+    rows = effects_ref.shape[0] // pieces
+    copies = [pltpu.make_async_copy(stacked_ref, stacked_out, sems.at[pieces])]
+    for p in range(pieces):
+        part = pl.ds(p * rows, rows)
+        copies.append(
+            pltpu.make_async_copy(effects_ref.at[part], effects_out.at[part], sems.at[p])
+        )
+    for copy in copies:
+        copy.start()
+    for copy in copies:
+        copy.wait()
 
 
 def row_block(strip):
@@ -489,7 +508,7 @@
                 transcendentals=0,
             ),
         )
-        return call(
+        effects, stacked = call(
             effects_start,
             marginal,
             ld_diag,
@@ -499,6 +518,18 @@
             dosages,
             stack_weights,
         )
+        return pl.pallas_call(
+            hand_out,
+            out_shape=(
+                jax.ShapeDtypeStruct(effects.shape, f32),
+                jax.ShapeDtypeStruct(stacked.shape, f32),
+            ),
+            in_specs=[anywhere] * 2,
+            out_specs=(anywhere, anywhere),
+            scratch_shapes=[dma((math.gcd(strip // 8, 8) + 1,))],
+            compiler_params=pltpu.CompilerParams(vmem_limit_bytes=60 * 2**20),
+        )(effects, stacked)
+
     return jax.shard_map(
         shards,
         mesh=mesh,

time: 56.6 us -> 72.2 us (1.28)
  Pallas kernels: 53.3 us -> 71.4 us
  local copies, waits for them, and re-layouts: 2.45 us -> 0 us
    pallas_call x0 -> x1, Pallas kernels: none -> 17.1 us  [shards(): pl.pallas_call(hand_out, out_shape=(jax.ShapeDtypeStruct(effects.shape, f...]
    unnamed x4 -> x0, local copies, waits for them, and re-layouts: 2.45 us -> none
    pallas_call x1, Pallas kernels: 53.3 us -> 54.3 us  [shards(): call(effects_start, marginal, ld_diag, ld_upper, penalty_grid[None, :], p...]
where the time goes in v4:
time: 72.2 us; the launch traced here: 72 us
  Pallas kernels  71.4 us (99%)
    pallas_call x1, Pallas kernels, shards(): call(effects_start, marginal, ld_diag, ld_upper, penalty_grid[None, :], p...  54.3 us
    pallas_call x1, Pallas kernels, shards(): pl.pallas_call(hand_out, out_shape=(jax.ShapeDtypeStruct(effects.shape, f...  17.1 us

profile of v4, /device:TPU:0, one launch (start us, length us, event | category | flops | bytes accessed | tf_op | source)
XLA Modules:
  0.0 72.0 jit_solution(13956476712211829545)
XLA Ops:
  0.6 54.3 %shard_map.95 = (f32[512,256]{1,0:T(8,128)}, f32[2,256]{1,0:T(2,128)}) custom-call(f32[512,256]{1,0:T(8,128)} %start_ref.1, f32[512,256]{1,0:T(8,128)} %marginal_ref.1, f32[512,512]{1,0:T(8,128)} %diag_ref.1, f32[512,512]{1,0:T(8,128)} %upper_ref.1, f32[1,16]{1,0:T(1,128)} %bitcast.3, s32[1,256]{1,0:T(1,128)} %bitcast.2, bf16[64,512]{1,0:T(8,128)(2,1)} %dosages_ref.1, ...), custom_call_target="tpu_custom_call" | custom-call | flops 3623878656 | bytes 3670016 | tf_op jit(solution)/shard_map/pallas_call | solution.py:511
  54.9 17.1 %shard_map.96 = (f32[512,256]{1,0:T(8,128)}, f32[2,256]{1,0:T(2,128)}) custom-call(f32[512,256]{1,0:T(8,128)} %get-tuple-element.4.effects_ref, f32[2,256]{1,0:T(2,128)} %get-tuple-element.5.stacked_ref), custom_call_target="tpu_custom_call" | custom-call | tf_op jit(solution)/shard_map/pallas_call | solution.py:521
